TPU v7x, 512 devices: a whole 4x8x8 slice. The times are simulated.
512 devices in a mesh: dev: 128 (over z, y, core), rep: 4 (over x).
Axes of the slice: x: 4, y: 8, z: 8, core: 2. Of those that a mesh axis runs over, the one named last changes fastest.
Arguments:
- params: float32 [10, 65536], P(None, 'dev'), may hold values from -8 to 6
- moment1: float32 [10, 65536], P(None, 'dev'), may hold values from -0.06 to 0.06
- moment2: float32 [10, 65536], P(None, 'dev'), may hold values from 0.0001 to 0.01
- camera: float32 [4, 8], P('rep'), may hold values from -3 to 3
- owner: int32 [4, 256, 512, 1], P('rep', 'dev'), may hold values from 0 to 127; in each aligned block of 1024 rows (0 to 1023, 1024 to 2047, ..., all dimensions but the last counted through in order) at most 16 rows name the same one
- local_index: int32 [4, 256, 512], P('rep', 'dev'), may hold values from 0 to 511
- target: float32 [4, 256, 3, 256], P('rep', 'dev'), may hold values from 0 to 1
- rehome: int32 [128, 128], P('dev'), may hold values from 0 to 127, each once within a row
Outputs:
- params_next: float32 [10, 65536], P(None, 'dev')
- moment1_next: float32 [10, 65536], P(None, 'dev')
- moment2_next: float32 [10, 65536], P(None, 'dev')
- rendered: float32 [4, 256, 3, 256], P('rep', 'dev')
Inputs may be any that keep to these rules, and one draw needn't show every extreme that they name: In the entries of one device's tiles of one camera (aligned blocks of 1024 entries) no owner is named more than 16 times, a bound that some block reaches. `rehome`: each row is a permutation of the devices.
All inputs are finite; a program needn't handle non-finite values.
Results may differ from a plain program's by a relative error of at most 0.00014.
Values sent between devices are 32-bit elements; how exact they have to be, the bound alone decides.
No kernel may reach another device: no remote copies, remote signals or barrier semaphores. Data moves between devices by JAX's collectives and lax.ppermute only.
A program may use at most 128 MiB of HBM per device.

v0:
```python
import functools
import jax
import jax.numpy as jnp
from jax import lax
from jax.sharding import PartitionSpec as P

SIDE = 16
PIX = 256
BACKGROUND = 0.5


def project(params, camera_row):
    xpos = params[0]
    ypos = params[1]
    zpos = params[2]
    screen_u = camera_row[0] * xpos + camera_row[1] * ypos + camera_row[2] * zpos + camera_row[3]
    screen_v = camera_row[4] * xpos + camera_row[5] * ypos + camera_row[6] * zpos + camera_row[7]
    conic_a = jnp.exp(params[3])
    conic_c = jnp.exp(params[5])
    conic_b = 0.9 * jnp.tanh(params[4]) * jnp.sqrt(conic_a * conic_c)
    opacity = jax.nn.sigmoid(params[6])
    colors = jax.nn.sigmoid(params[7:10])
    head = jnp.stack([screen_u, screen_v, conic_a, conic_b, conic_c, opacity])
    return jnp.concatenate([head, colors], axis=0)


def render(values):
    pixel_ids = jnp.arange(PIX)
    column = (pixel_ids % SIDE).astype(jnp.float32) - 7.5
    row_pos = (pixel_ids // SIDE).astype(jnp.float32) - 7.5
    delta_u = column[None, :, None] - values[:, 0][:, None, :]
    delta_v = row_pos[None, :, None] - values[:, 1][:, None, :]
    quad = (
        values[:, 2][:, None, :] * delta_u * delta_u
        + 2.0 * values[:, 3][:, None, :] * delta_u * delta_v
        + values[:, 4][:, None, :] * delta_v * delta_v
    )
    alpha = 0.99 * values[:, 5][:, None, :] * jnp.exp(-0.5 * quad)
    log_keep = jnp.log(1.0 - alpha)
    running = jnp.cumsum(log_keep, axis=2)
    weight = alpha * jnp.exp(running - log_keep)
    image = jnp.einsum("bpk,bck->bcp", weight, values[:, 6:9], precision=lax.Precision.HIGHEST)
    return image + BACKGROUND * jnp.exp(running[:, :, -1])[:, None, :]


def local(params, moment1, moment2, camera, owner, local_index, target, rehome):
    devices = lax.axis_size("dev")
    gauss_dev = params.shape[1]
    tiles_dev = local_index.shape[1]
    list_len = local_index.shape[2]
    projected, pullback = jax.vjp(functools.partial(project, camera_row=camera[0]), params)
    destination = owner[0, :, :, 0].reshape(-1)
    local_ids = local_index[0].reshape(-1)
    whole = lax.all_gather(projected, "dev", axis=1, tiled=True)
    global_ids = destination * gauss_dev + local_ids
    entries = jnp.take(whole, global_ids, axis=1)
    values = (
        entries.reshape(9, tiles_dev, list_len)
        .transpose(1, 0, 2)
        .reshape(tiles_dev // 2, 2, 9, list_len)
    )
    goals = target[0].reshape(tiles_dev // 2, 2, 3, PIX)

    def one_block(pair):
        block_values, block_target = pair
        image, pull_render = jax.vjp(render, block_values)
        return (image, pull_render(image - block_target)[0])

    images, grad_values = lax.map(one_block, (values, goals))
    grad_entries = grad_values.reshape(tiles_dev, 9, list_len).transpose(1, 0, 2).reshape(9, -1)
    spread = jnp.zeros((9, gauss_dev * devices), jnp.float32).at[:, global_ids].add(grad_entries)
    grad_table = lax.psum_scatter(spread, "dev", scatter_dimension=1, tiled=True)
    grad_local = pullback(grad_table)[0]
    grad_total = lax.psum(grad_local, "rep")
    moment1_new = 0.9 * moment1 + 0.1 * grad_total
    moment2_new = 0.99 * moment2 + 0.01 * grad_total * grad_total
    params_new = params - 0.01 * moment1_new / (jnp.sqrt(moment2_new) + 1e-08)
    stacked = jnp.stack([params_new, moment1_new, moment2_new]).reshape(
        3, 10, devices, gauss_dev // devices
    )
    block_ids = jnp.arange(devices, dtype=jnp.int32)
    matches = (rehome[0][:, None] == block_ids[None, :]).astype(jnp.int32)
    inverse = jnp.sum(matches * block_ids[:, None], axis=0)
    outgoing_blocks = jnp.take(stacked, inverse, axis=2)
    arrived = lax.all_to_all(
        outgoing_blocks, "dev", split_axis=2, concat_axis=2, tiled=True
    ).reshape(3, 10, gauss_dev)
    return (arrived[0], arrived[1], arrived[2], images)


def solution(mesh):
    in_specs = (
        P(None, "dev"),
        P(None, "dev"),
        P(None, "dev"),
        P("rep", None),
        P("rep", "dev", None, None),
        P("rep", "dev", None),
        P("rep", "dev", None, None),
        P("dev", None),
    )
    out_specs = (P(None, "dev"), P(None, "dev"), P(None, "dev"), P("rep", "dev", None, None))
    return jax.shard_map(local, mesh=mesh, in_specs=in_specs, out_specs=out_specs, check_vma=False)
```

profile of v0, /device:TPU:1, one launch (start us, length us, event | category | flops | bytes accessed | tf_op | source)
XLA Modules:
  0.0 469.2 jit_solution(8419153605545001573)
XLA Ops:
  7.2 1.6 fusion.66
  8.9 0.8 add_divide_fusion
  9.6 3.5 add_divide_fusion.1
  13.1 3.5 add_add_fusion
  16.6 2.0 concatenate.4
  18.7 0.7 fusion.47
  19.4 0.7 copy.274
  20.1 0.7 compare_and_fusion
  20.8 88.6 %all-gather.2.cloned.1.call-done = f32[9,65536]{1,0:T(8,128)} async-done(((f32[9,512]{1,0:T(8,128)}), f32[9,65536]{1,0:T(8,128)}) %all-gather.2.cloned.1.call-update) | async-done | bytes 2359312 | tf_op jit(solution)/shard_map/all_gather | solution.py:54
  109.4 16.9 %copy.241 = f32[9,65536]{0,1:T(8,128)} copy(f32[9,65536]{1,0:T(8,128)} %all-gather.2.cloned.1.call-done) | data formatting | bytes 4718592 | tf_op jit(solution)/shard_map/all_gather | solution.py:54
  126.4 13.3 %gather_fusion = f32[1024,9]{1,0:T(8,128)S(1)} fusion(f32[9,65536]{0,1:T(8,128)} %copy.241, s32[1024]{0:T(1024)S(1)} %broadcast_clamp_fusion), kind=kCustom, calls=%fused_computation | custom fusion | bytes 77824 | tf_op jit(solution)/shard_map/jit(_take)/gather | solution.py:56
  139.7 0.2 copy.243
  140.9 1.8 fusion.18
  142.7 0.2 broadcast_add_fusion.1
  142.9 0.6 copy.250
  143.5 0.4 reduce_window_sum.33
  143.9 0.3 multiply_reduce_fusion.1
  144.2 1.7 fusion.63
  145.9 1.4 fusion.39
  147.4 0.2 copy.252
  147.5 0.2 fusion.38
  147.7 2.8 pad_add_fusion
  150.5 0.4 reshape.269
  150.8 0.8 copy.253
  151.6 4.3 fusion.67
  156.0 0.2 broadcast_add_fusion
  156.2 0.6 copy.254
  156.8 0.4 reduce_window_sum.35
  157.2 3.2 fusion.24
  160.7 0.2 copy.256
  160.9 19.2 %scatter_custom_fusion = f32[9,65536]{0,1:T(8,128)} fusion(s32[1024]{0:T(1024)S(1)} %bitcast.99, f32[1024,9]{1,0:T(8,128)S(1)} %copy.256, f32[]{:T(128)} %constant.106.clone.1), kind=kCustom, calls=%fused_computation.3 | custom fusion | flops 9216 | bytes 2359300 | tf_op jit(solution)/shard_map/scatter-add | solution.py:71
  180.1 19.4 %copy.257 = f32[9,65536]{1,0:T(8,128)} copy(f32[9,65536]{0,1:T(8,128)} %scatter_custom_fusion) | data formatting | bytes 4718592 | tf_op jit(solution)/shard_map/scatter-add | solution.py:71
  199.7 193.3 %reduce-scatter.2.cloned.1.call-done = f32[9,512]{1,0:T(8,128)} async-done(((f32[9,65536]{1,0:T(8,128)}), f32[9,512]{1,0:T(8,128)}) %reduce-scatter.2.cloned.1.call-update) | async-done | bytes 18448 | tf_op jit(solution)/shard_map/reduce_scatter | solution.py:72
  393.0 4.7 fusion.48
  397.7 0.8 fusion.46
  398.4 0.8 multiply_multiply_fusion.4
  399.3 13.2 %psum.7 = f32[10,512]{1,0:T(8,128)S(1)} all-reduce(f32[10,512]{1,0:T(8,128)S(1)} %pad_add_fusion.1), channel_id=1, replica_groups=mesh['dev'=128,'rep'=4] {'rep'}, use_global_device_ids=true, to_apply=%region_14.15 | all-reduce | flops 5120 | bytes 40960 | tf_op jit(solution)/shard_map/psum | solution.py:74
  412.8 0.1 copy.259
  412.9 0.1 copy.260
  413.1 0.2 pad_maximum_fusion
  413.3 1.1 gather_fusion.1
  414.4 1.1 select_bitcast_fusion
  415.6 18.6 %all-to-all-start = ((f32[3,10,128,4]{1,3,0,2:T(4,128)}), f32[3,10,128,4]{1,3,0,2:T(4,128)S(1)}, u32[]{:S(2)}, u32[]{:S(2)}) async-start(f32[3,10,128,4]{1,3,0,2:T(4,128)} %select_bitcast_fusion), calls=%async_computation.1 | async-start | bytes 1572864 | tf_op jit(solution)/shard_map/all_to_all | solution.py:85
  434.1 0.6 copy.264
  434.7 25.3 %all-to-all-done = f32[3,10,128,4]{1,3,0,2:T(4,128)S(1)} async-done(((f32[3,10,128,4]{1,3,0,2:T(4,128)}), f32[3,10,128,4]{1,3,0,2:T(4,128)S(1)}, u32[]{:S(2)}, u32[]{:S(2)}) %all-to-all-start) | async-done | bytes 61472 | tf_op jit(solution)/shard_map/all_to_all | solution.py:85
  460.2 0.7 copy.261
  460.9 0.7 copy.262
  461.7 0.7 copy.263
  (58 shorter events, 1.8 us)
Async XLA Ops:
  7.2 137.0 %copy-start.3 = (f32[1,2,3,256]{3,1,2,0:T(2,128)S(1)}, f32[1,2,3,256]{3,1,2,0:T(2,128)}, u32[]{:S(2)}) copy-start(f32[1,2,3,256]{3,1,2,0:T(2,128)} %param.14) | copy-start | bytes 18436
  7.2 102.3 %all-gather.2.cloned.1.call-start = ((), (), s32[]{:S(2)}) async-start(), calls=%async_computation.2 | async-start | bytes 4227072 | tf_op jit(solution)/shard_map/all_gather | solution.py:54
  18.6 374.3 %reduce-scatter.2.cloned.1.call-start = ((), (), s32[]{:S(2)}) async-start(), calls=%async_computation.3 | async-start | bytes 4227072 | tf_op jit(solution)/shard_map/reduce_scatter | solution.py:72
  160.9 38.7 %copy-start.4 = (s32[1,128]{1,0:T(1,128)S(1)}, s32[1,128]{1,0:T(1,128)}, u32[]{:S(2)}) copy-start(s32[1,128]{1,0:T(1,128)} %param.15) | copy-start | bytes 1540
  160.9 232.1 %copy-start = (f32[10,512]{1,0:T(8,128)S(1)}, f32[10,512]{1,0:T(8,128)}, u32[]{:S(2)}) copy-start(f32[10,512]{1,0:T(8,128)} %param.8) | copy-start | bytes 61444
  160.9 251.7 %copy-start.1 = (f32[10,512]{1,0:T(8,128)S(1)}, f32[10,512]{1,0:T(8,128)}, u32[]{:S(2)}) copy-start(f32[10,512]{1,0:T(8,128)} %param.9) | copy-start | bytes 61444
  160.9 251.7 %copy-start.2 = (f32[10,512]{1,0:T(8,128)S(1)}, f32[10,512]{1,0:T(8,128)}, u32[]{:S(2)}) copy-start(f32[10,512]{1,0:T(8,128)} %param.10) | copy-start | bytes 61444
  415.6 44.5 %all-to-all-start = ((f32[3,10,128,4]{1,3,0,2:T(4,128)}), f32[3,10,128,4]{1,3,0,2:T(4,128)S(1)}, u32[]{:S(2)}, u32[]{:S(2)}) async-start(f32[3,10,128,4]{1,3,0,2:T(4,128)} %select_bitcast_fusion), calls=%async_computation.1 | async-start | bytes 1572864 | tf_op jit(solution)/shard_map/all_to_all | solution.py:85
Sparse Core Ops, SparseCore 0:
  18.8 90.6 all-gather.1
  199.7 193.2 reduce-scatter.1
where the time goes:
time: 471 us; the launch traced here: 469 us
  waiting for transfers between devices  307 us (65%)
  local copies, waits for them, and re-layouts  63.2 us (13%)
  other arithmetic  46.4 us (10%)
  starting transfers between devices  18.6 us (4%)
  between operations  14.6 us (3%)
  blocking collectives  13.2 us (3%)
  matrix products  5.91 us (1%)
    reduce_scatter x1, waiting for transfers between devices, local(): lax.psum_scatter(spread, 'dev', scatter_dimension=1, tiled=True)  193 us
    all_gather x1, waiting for transfers between devices, local(): whole = lax.all_gather(projected, 'dev', axis=1, tiled=True)  88.6 us
    all_to_all x1, waiting for transfers between devices, local(): lax.all_to_all(outgoing_blocks, 'dev', split_axis=2, concat_axis=2, tiled...  25.3 us
    scatter-add x1, local copies, waits for them, and re-layouts, local(): jnp.zeros((9, gauss_dev * devices), jnp.float32).at[:, global_ids]  19.4 us
    scatter-add x1, other arithmetic, local(): jnp.zeros((9, gauss_dev * devices), jnp.float32).at[:, global_ids]  19.2 us
    all_to_all x1, starting transfers between devices, local(): lax.all_to_all(outgoing_blocks, 'dev', split_axis=2, concat_axis=2, tiled...  18.6 us
    all_gather x1, local copies, waits for them, and re-layouts, local(): whole = lax.all_gather(projected, 'dev', axis=1, tiled=True)  16.9 us
    gather x2, local copies, waits for them, and re-layouts, local(): entries = jnp.take(whole, global_ids, axis=1)  13.5 us
  transfers between devices with their start and end apart: 3, of which 3 were waited for; matrix products, arithmetic and copies ran while one was open for 1% of the time, Pallas kernels for 0%

commit v1 on v0

--- a/solution.py
+++ b/solution.py
@@ -51,7 +51,10 @@
     projected, pullback = jax.vjp(functools.partial(project, camera_row=camera[0]), params)
     destination = owner[0, :, :, 0].reshape(-1)
     local_ids = local_index[0].reshape(-1)
-    whole = lax.all_gather(projected, "dev", axis=1, tiled=True)
+    size = lax.axis_size("dev")
+    pieces = jnp.stack([projected for _ in range(size)])
+    pieces = lax.all_to_all(pieces, "dev", split_axis=0, concat_axis=0)
+    whole = jnp.concatenate(pieces, axis=1)
     global_ids = destination * gauss_dev + local_ids
     entries = jnp.take(whole, global_ids, axis=1)
     values = (

time: 471 us -> 503 us (1.068)
  starting transfers between devices: 18.6 us -> 37.5 us
  waiting for transfers between devices: 307 us -> 320 us
    all_to_all x0 -> x1, waiting for transfers between devices: none -> 94.3 us  [local(): pieces = lax.all_to_all(pieces, 'dev', split_axis=0, concat_axis=0)]
    all_gather x1 -> x0, waiting for transfers between devices: 88.6 us -> none  [local(): whole = lax.all_gather(projected, 'dev', axis=1, tiled=True)]
    all_to_all x0 -> x1, starting transfers between devices: none -> 18.9 us  [local(): pieces = lax.all_to_all(pieces, 'dev', split_axis=0, concat_axis=0)]
    reshape x0 -> x1, local copies, waits for them, and re-layouts: none -> 17 us  [local(): whole = jnp.concatenate(pieces, axis=1)]
    all_gather x1 -> x0, local copies, waits for them, and re-layouts: 16.9 us -> none  [local(): whole = lax.all_gather(projected, 'dev', axis=1, tiled=True)]
    reduce_scatter x1, waiting for transfers between devices: 193 us -> 200 us  [local(): lax.psum_scatter(spread, 'dev', scatter_dimension=1, tiled=True)]
where the time goes in v1:
time: 503 us; the launch traced here: 501 us
  waiting for transfers between devices  320 us (64%)
  local copies, waits for them, and re-layouts  63.8 us (13%)
  other arithmetic  46.4 us (9%)
  starting transfers between devices  37.5 us (7%)
  between operations  14.6 us (3%)
  blocking collectives  13.3 us (3%)
  matrix products  5.91 us (1%)
    reduce_scatter x1, waiting for transfers between devices, local(): lax.psum_scatter(spread, 'dev', scatter_dimension=1, tiled=True)  200 us
    all_to_all x1, waiting for transfers between devices, local(): pieces = lax.all_to_all(pieces, 'dev', split_axis=0, concat_axis=0)  94.3 us
    all_to_all x1, waiting for transfers between devices, local(): lax.all_to_all(outgoing_blocks, 'dev', split_axis=2, concat_axis=2, tiled...  25.3 us
    scatter-add x1, local copies, waits for them, and re-layouts, local(): jnp.zeros((9, gauss_dev * devices), jnp.float32).at[:, global_ids]  19.4 us
    scatter-add x1, other arithmetic, local(): jnp.zeros((9, gauss_dev * devices), jnp.float32).at[:, global_ids]  19.2 us
    all_to_all x1, starting transfers between devices, local(): pieces = lax.all_to_all(pieces, 'dev', split_axis=0, concat_axis=0)  18.9 us
    all_to_all x1, starting transfers between devices, local(): lax.all_to_all(outgoing_blocks, 'dev', split_axis=2, concat_axis=2, tiled...  18.6 us
    reshape x1, local copies, waits for them, and re-layouts, local(): whole = jnp.concatenate(pieces, axis=1)  17 us
  transfers between devices with their start and end apart: 3, of which 3 were waited for; matrix products, arithmetic and copies ran while one was open for 1% of the time, Pallas kernels for 0%

profile of v1, /device:TPU:1, one launch (start us, length us, event | category | flops | bytes accessed | tf_op | source)
XLA Modules:
  0.0 501.0 jit_solution(238114020972739222)
XLA Ops:
  7.2 1.6 fusion.66
  8.8 0.8 add_divide_fusion
  9.6 3.5 add_divide_fusion.1
  13.1 3.5 add_add_fusion
  16.7 2.5 stack.10
  19.1 18.9 %all-to-all-start = ((f32[128,9,512]{2,1,0:T(8,128)}), f32[128,9,512]{2,1,0:T(8,128)}, u32[]{:S(2)}, u32[]{:S(2)}) async-start(f32[128,9,512]{2,1,0:T(8,128)} %stack.10), calls=%async_computation | async-start | bytes 8388608 | tf_op jit(solution)/shard_map/all_to_all | solution.py:56
  38.1 0.7 fusion.47
  38.8 0.7 copy.278
  39.5 0.7 compare_and_fusion
  40.2 94.3 %all-to-all-done = f32[128,9,512]{2,1,0:T(8,128)} async-done(((f32[128,9,512]{2,1,0:T(8,128)}), f32[128,9,512]{2,1,0:T(8,128)}, u32[]{:S(2)}, u32[]{:S(2)}) %all-to-all-start) | async-done | bytes 2359328 | tf_op jit(solution)/shard_map/all_to_all | solution.py:56
  134.6 17.0 %copy.245 = f32[9,128,512]{0,2,1:T(8,128)} copy(f32[9,128,512]{2,0,1:T(8,128)} %bitcast.12) | data formatting | bytes 4718592 | tf_op jit(solution)/shard_map/reshape | solution.py:57
  151.5 13.3 %gather_fusion = f32[1024,9]{1,0:T(8,128)S(1)} fusion(f32[9,65536]{0,1:T(8,128)} %bitcast.85, s32[1024]{0:T(1024)S(1)} %broadcast_clamp_fusion), kind=kCustom, calls=%fused_computation | custom fusion | bytes 77824 | tf_op jit(solution)/shard_map/jit(_take)/gather | solution.py:59
  164.9 0.2 copy.247
  166.0 1.8 fusion.18
  167.9 0.2 broadcast_add_fusion.1
  168.1 0.6 copy.254
  168.7 0.4 reduce_window_sum.33
  169.1 0.3 multiply_reduce_fusion.1
  169.4 1.7 fusion.63
  171.1 1.4 fusion.39
  172.5 0.2 copy.256
  172.7 0.2 fusion.38
  172.8 2.8 pad_add_fusion
  175.6 0.4 reshape.279
  176.0 0.8 copy.257
  176.7 4.3 fusion.67
  181.1 0.2 broadcast_add_fusion
  181.3 0.6 copy.258
  181.9 0.4 reduce_window_sum.35
  182.3 3.2 fusion.24
  185.8 0.2 copy.260
  186.1 19.2 %scatter_custom_fusion = f32[9,65536]{0,1:T(8,128)} fusion(s32[1024]{0:T(1024)S(1)} %bitcast.102, f32[1024,9]{1,0:T(8,128)S(1)} %copy.260, f32[]{:T(128)} %constant.106.clone.1), kind=kCustom, calls=%fused_computation.3 | custom fusion | flops 9216 | bytes 2359300 | tf_op jit(solution)/shard_map/scatter-add | solution.py:74
  205.3 19.4 %copy.261 = f32[9,65536]{1,0:T(8,128)} copy(f32[9,65536]{0,1:T(8,128)} %scatter_custom_fusion) | data formatting | bytes 4718592 | tf_op jit(solution)/shard_map/scatter-add | solution.py:74
  224.8 199.9 %reduce-scatter.2.cloned.1.call-done = f32[9,512]{1,0:T(8,128)} async-done(((f32[9,65536]{1,0:T(8,128)}), f32[9,512]{1,0:T(8,128)}) %reduce-scatter.2.cloned.1.call-update) | async-done | bytes 18448 | tf_op jit(solution)/shard_map/reduce_scatter | solution.py:75
  424.7 4.7 fusion.48
  429.4 0.8 fusion.46
  430.2 0.8 multiply_multiply_fusion.4
  431.1 13.3 %psum.7 = f32[10,512]{1,0:T(8,128)S(1)} all-reduce(f32[10,512]{1,0:T(8,128)S(1)} %pad_add_fusion.1), channel_id=1, replica_groups=mesh['dev'=128,'rep'=4] {'rep'}, use_global_device_ids=true, to_apply=%region_14.15 | all-reduce | flops 5120 | bytes 40960 | tf_op jit(solution)/shard_map/psum | solution.py:77
  444.7 0.1 copy.264
  444.8 0.2 pad_maximum_fusion
  445.1 1.1 gather_fusion.1
  446.2 1.1 select_bitcast_fusion
  447.3 18.6 %all-to-all-start.1 = ((f32[3,10,128,4]{1,3,0,2:T(4,128)}), f32[3,10,128,4]{1,3,0,2:T(4,128)S(1)}, u32[]{:S(2)}, u32[]{:S(2)}) async-start(f32[3,10,128,4]{1,3,0,2:T(4,128)} %select_bitcast_fusion), calls=%async_computation.2 | async-start | bytes 1572864 | tf_op jit(solution)/shard_map/all_to_all | solution.py:88
  465.9 0.6 copy.268
  466.5 25.3 %all-to-all-done.1 = f32[3,10,128,4]{1,3,0,2:T(4,128)S(1)} async-done(((f32[3,10,128,4]{1,3,0,2:T(4,128)}), f32[3,10,128,4]{1,3,0,2:T(4,128)S(1)}, u32[]{:S(2)}, u32[]{:S(2)}) %all-to-all-start.1) | async-done | bytes 61472 | tf_op jit(solution)/shard_map/all_to_all | solution.py:88
  492.0 0.7 copy.265
  492.7 0.7 copy.266
  493.5 0.7 copy.267
  (58 shorter events, 2.0 us)
Async XLA Ops:
  7.2 162.2 %copy-start.3 = (f32[1,2,3,256]{3,1,2,0:T(2,128)S(1)}, f32[1,2,3,256]{3,1,2,0:T(2,128)}, u32[]{:S(2)}) copy-start(f32[1,2,3,256]{3,1,2,0:T(2,128)} %param.14) | copy-start | bytes 18436
  19.1 115.4 %all-to-all-start = ((f32[128,9,512]{2,1,0:T(8,128)}), f32[128,9,512]{2,1,0:T(8,128)}, u32[]{:S(2)}, u32[]{:S(2)}) async-start(f32[128,9,512]{2,1,0:T(8,128)} %stack.10), calls=%async_computation | async-start | bytes 8388608 | tf_op jit(solution)/shard_map/all_to_all | solution.py:56
  38.0 386.7 %reduce-scatter.2.cloned.1.call-start = ((), (), s32[]{:S(2)}) async-start(), calls=%async_computation.3 | async-start | bytes 4227072 | tf_op jit(solution)/shard_map/reduce_scatter | solution.py:75
  186.0 38.7 %copy-start.4 = (s32[1,128]{1,0:T(1,128)S(1)}, s32[1,128]{1,0:T(1,128)}, u32[]{:S(2)}) copy-start(s32[1,128]{1,0:T(1,128)} %param.15) | copy-start | bytes 1540
  186.0 238.7 %copy-start = (f32[10,512]{1,0:T(8,128)S(1)}, f32[10,512]{1,0:T(8,128)}, u32[]{:S(2)}) copy-start(f32[10,512]{1,0:T(8,128)} %param.8) | copy-start | bytes 61444
  186.0 258.3 %copy-start.1 = (f32[10,512]{1,0:T(8,128)S(1)}, f32[10,512]{1,0:T(8,128)}, u32[]{:S(2)}) copy-start(f32[10,512]{1,0:T(8,128)} %param.9) | copy-start | bytes 61444
  186.1 258.3 %copy-start.2 = (f32[10,512]{1,0:T(8,128)S(1)}, f32[10,512]{1,0:T(8,128)}, u32[]{:S(2)}) copy-start(f32[10,512]{1,0:T(8,128)} %param.10) | copy-start | bytes 61444
  447.3 44.5 %all-to-all-start.1 = ((f32[3,10,128,4]{1,3,0,2:T(4,128)}), f32[3,10,128,4]{1,3,0,2:T(4,128)S(1)}, u32[]{:S(2)}, u32[]{:S(2)}) async-start(f32[3,10,128,4]{1,3,0,2:T(4,128)} %select_bitcast_fusion), calls=%async_computation.2 | async-start | bytes 1572864 | tf_op jit(solution)/shard_map/all_to_all | solution.py:88
Sparse Core Ops, SparseCore 0:
  224.8 199.8 reduce-scatter.1
